TPU v7x, 32 devices: a whole 2x2x4 slice. The times are simulated.
32 devices in a mesh: tiles: 16 (over z, y, x), lev: 2 (over core).
Axes of the slice: x: 2, y: 2, z: 4, core: 2. Of those that a mesh axis runs over, the one named last changes fastest.
Arguments:
- atm_anom: bfloat16 [16, 30, 65536], P('lev', None, 'tiles'), may hold values from -6 to 6
- ocn_anom: bfloat16 [20, 30, 393216], P('lev', None, 'tiles'), may hold values from -6 to 6
- remap_w: bfloat16 [1024, 128, 128], P('tiles'), may hold values from -0.5 to 0.5
- rem_tile: int32 [1024, 1], P('tiles'), may hold values from 0 to 15; in each aligned block of 64 rows (0 to 63, 64 to 127, ...) at most 8 rows name the same one
- rem_block: int32 [1024], P('tiles'), may hold values from 0 to 191
- obs_weight: bfloat16 [16, 393216], P('lev', 'tiles'), may hold values from -1.5 to 1.5
- innov_ocn: float32 [393216], P('tiles'), may hold values from -6 to 6
- innov_atm: float32 [65536], P('tiles'), may hold values from -6 to 6
- band_ocn: int32 [393216], P('tiles'), may hold values from 0 to 19
- band_atm: int32 [65536], P('tiles'), may hold values from 0 to 15
Outputs:
- ocn_increment: float32 [20, 393216], P('lev', 'tiles')
- atm_increment: float32 [16, 65536], P('lev', 'tiles')
Inputs may be any that keep to these rules, and one draw needn't show every extreme that they name: `rem_tile`: in each tile's 64 remap blocks no ocean tile is named more than 8 times, a bound that some block reaches.
All inputs are finite; a program needn't handle non-finite values.
Results may differ from a plain program's by a relative error of at most 0.003.
Values may be sent and summed in bfloat16 or wider, within the bound.
A program may use at most 128 MiB of HBM per device.

v0:
```python
import jax
import jax.numpy as jnp
from jax import lax
from jax.sharding import PartitionSpec as P

MEM = 30
OLEV = 20
LTAP = 8


def taper_levels(first, levels, band):
    lvl = (first + jnp.arange(levels, dtype=jnp.int32)).astype(jnp.float32)[:, None]
    return jnp.maximum(0.0, 1.0 - jnp.abs(lvl - band[None, :].astype(jnp.float32)) / LTAP)


def increment(anom, proj, tapered, innov):
    cov = jnp.sum(anom.astype(jnp.float32) * proj[None], axis=1) / (MEM - 1)
    var = jnp.sum(proj * proj, axis=0) / (MEM - 1) + 0.1
    return tapered * cov * (innov / var)[None, :]


def shards(
    atm_anom,
    ocn_anom,
    remap_w,
    rem_tile,
    rem_block,
    obs_weight,
    innov_ocn,
    innov_atm,
    band_ocn,
    band_atm,
):
    ntiles = lax.axis_size("tiles")
    level_rank = lax.axis_index("lev")
    alev_loc, members, acells = atm_anom.shape
    olev_loc = ocn_anom.shape[0]
    ocells = ocn_anom.shape[2]
    ablk = acells // 128
    oblk = ocells // 128
    nrem = remap_w.shape[0]
    rpb = nrem // ablk
    per_owner = max(2, 2 * ((nrem + ntiles - 1) // ntiles))
    slots = ntiles * per_owner
    rows = alev_loc * members
    blocks = (
        atm_anom.reshape(alev_loc, members, ablk, 128)
        .transpose(2, 0, 1, 3)
        .reshape(ablk, rows, 128)
    )
    source = jnp.repeat(blocks, rpb, axis=0)
    dest = rem_tile[:, 0]
    match_dest = (dest[:, None] == jnp.arange(ntiles, dtype=jnp.int32)[None, :]).astype(jnp.int32)
    rank = jnp.sum(jnp.cumsum(match_dest, axis=0) * match_dest, axis=1) - 1
    slot_of = dest * per_owner + rank
    match_slot = (slot_of[None, :] == jnp.arange(slots, dtype=jnp.int32)[:, None]).astype(jnp.int32)
    filled = jnp.sum(match_slot, axis=1)
    slot_src = jnp.sum(match_slot * jnp.arange(nrem, dtype=jnp.int32)[None, :], axis=1)
    send_blk = jnp.where(filled > 0, rem_block[slot_src], -1)
    keep = filled.astype(jnp.bfloat16)[:, None, None]
    layer_part = jnp.sum(ocn_anom.astype(jnp.float32), axis=0) / OLEV
    layer_mean = lax.psum(layer_part, "lev")
    remapped = jnp.einsum(
        "irc,icd->ird", source, remap_w, preferred_element_type=jnp.float32
    ).astype(jnp.bfloat16)
    sent = jnp.take(remapped, slot_src, axis=0) * keep
    arrived, arrived_blk = (
        lax.all_to_all(sent, "tiles", split_axis=0, concat_axis=0, tiled=True),
        lax.all_to_all(send_blk, "tiles", split_axis=0, concat_axis=0, tiled=True),
    )
    owner_hot = (arrived_blk[None, :] == jnp.arange(oblk, dtype=jnp.int32)[:, None]).astype(
        jnp.bfloat16
    )
    on_ocean = jnp.dot(
        owner_hot, arrived.reshape(slots, rows * 128), preferred_element_type=jnp.float32
    )
    on_ocean = on_ocean.reshape(oblk, alev_loc, members, 128)
    weight_loc = obs_weight.reshape(alev_loc, oblk, 128).transpose(1, 0, 2).astype(jnp.float32)
    proj_part = jnp.sum(on_ocean * weight_loc[:, :, None, :], axis=1)
    proj_part = proj_part.transpose(1, 0, 2).reshape(members, ocells)
    proj = lax.psum(proj_part, "lev")
    layer_blocks = layer_mean.astype(jnp.bfloat16).reshape(members, oblk, 128).transpose(1, 0, 2)
    answer = jnp.take(layer_blocks, jnp.maximum(arrived_blk, 0), axis=0)
    returned = lax.all_to_all(answer, "tiles", split_axis=0, concat_axis=0, tiled=True)
    mine = jnp.take(returned, slot_of, axis=0)
    atm_part = jnp.einsum("imd,icd->imc", mine, remap_w, preferred_element_type=jnp.float32)
    atm_part = atm_part.reshape(ablk, rpb, members, 128).sum(axis=1)
    ocn_on_atm = atm_part.transpose(1, 0, 2).reshape(members, acells)
    taper_ocn = taper_levels(level_rank * olev_loc, olev_loc, band_ocn)
    taper_atm = taper_levels(level_rank * alev_loc, alev_loc, band_atm)
    ocn_increment = increment(ocn_anom, proj, taper_ocn, innov_ocn)
    atm_increment = increment(atm_anom, ocn_on_atm, taper_atm, innov_atm)
    return (ocn_increment, atm_increment)


def solution(mesh):
    in_specs = (
        P("lev", None, "tiles"),
        P("lev", None, "tiles"),
        P("tiles", None, None),
        P("tiles", None),
        P("tiles"),
        P("lev", "tiles"),
        P("tiles"),
        P("tiles"),
        P("tiles"),
        P("tiles"),
    )
    out_specs = (P("lev", "tiles"), P("lev", "tiles"))
    return jax.shard_map(shards, mesh=mesh, in_specs=in_specs, out_specs=out_specs, check_vma=False)
```

profile of v0, /device:TPU:13, one launch (start us, length us, event | category | flops | bytes accessed | tf_op | source)
XLA Modules:
  0.0 362.2 jit_solution(11455464064673677382)
XLA Ops:
  7.2 0.0 copy-start
  7.2 0.9 fusion.10
  8.1 0.1 reduce_window_sum.11
  8.2 0.8 select_reduce_fusion.1
  9.0 0.7 multiply_add_fusion
  9.7 0.1 convert_reduce_fusion.1
  9.8 1.6 gather_fusion
  11.4 0.7 select_n.54
  12.1 6.6 %all-to-all-start = ((s32[16,8,1]{1,2,0:T(1,128)}), s32[16,8,1]{1,2,0:T(1,128)S(1)}, u32[]{:S(2)}, u32[]{:S(2)}) async-start(s32[16,8,1]{1,2,0:T(1,128)} %bitcast.3), calls=%async_computation | async-start | bytes 16384 | tf_op jit(solution)/shard_map/all_to_all | solution.py:69
  18.7 2.0 copy.54
  20.7 0.4 copy.37
  21.1 0.8 copy.38
  21.8 0.5 broadcast_in_dim.55
  22.4 0.0 copy-done
  22.4 4.1 %convolution_convert_fusion = bf16[64,240,128]{2,1,0:T(8,128)(2,1)} fusion(bf16[64,240,128]{2,1,0:T(8,128)(2,1)S(1)} %bitcast.72, bf16[64,128,128]{2,1,0:T(8,128)(2,1)S(1)} %copy-done), kind=kOutput, calls=%fused_computation.12 | convolution fusion | flops 505282560 | bytes 9961472 | tf_op jit(solution)/shard_map/irc,icd->ird/dot_general | solution.py:63
  26.4 8.6 %gather_fusion.1 = bf16[128,240,128]{2,1,0:T(8,128)(2,1)} fusion(bf16[64,240,128]{2,1,0:T(8,128)(2,1)} %convolution_convert_fusion, s32[1024]{0:T(1024)S(1)} %pad_clamp_fusion.2), kind=kCustom, calls=%fused_computation.1 | custom fusion | bytes 15729152 | tf_op jit(solution)/shard_map/jit(_take)/gather | solution.py:66
  35.0 7.2 %select_multiply_fusion = bf16[128,240,128]{2,1,0:T(8,128)(2,1)} fusion(bf16[128,240,128]{2,1,0:T(8,128)(2,1)} %gather_fusion.1, pred[128]{0:T(512)(128)(4,1)S(1)} %compare_and_fusion, bf16[128]{0:T(256)(128)(2,1)S(1)} %get-tuple-element.11), kind=kLoop, calls=%fused_computation.9 | loop fusion | flops 7864320 | bytes 15729024 | tf_op jit(solution)/shard_map/mul | solution.py:66
  42.3 0.0 copy-start.3
  42.3 0.0 all-to-all-done
  42.3 6.5 %all-to-all-start.1 = ((bf16[128,240,128]{2,1,0:T(8,128)(2,1)}), bf16[128,240,128]{2,1,0:T(8,128)(2,1)}, u32[]{:S(2)}, u32[]{:S(2)}) async-start(bf16[128,240,128]{2,1,0:T(8,128)(2,1)} %select_multiply_fusion), calls=%async_computation.1 | async-start | bytes 15728640 | tf_op jit(solution)/shard_map/all_to_all | solution.py:68
  48.8 0.2 all-reduce.3.cloned.1.call-start
  49.0 0.0 copy-done.3
  49.0 0.1 bitcast_convert_fusion
  49.1 0.2 copy.56
  49.2 0.5 broadcast.166
  49.7 0.7 maximum_reduce_fusion
  50.4 0.1 eq.47
  50.5 173.5 %all-to-all-done.1 = bf16[128,240,128]{2,1,0:T(8,128)(2,1)} async-done(((bf16[128,240,128]{2,1,0:T(8,128)(2,1)}), bf16[128,240,128]{2,1,0:T(8,128)(2,1)}, u32[]{:S(2)}, u32[]{:S(2)}) %all-to-all-start.1) | async-done | bytes 7864352 | tf_op jit(solution)/shard_map/all_to_all | solution.py:68
  224.0 8.4 %copy.53 = bf16[16,8,240,128]{3,1,2,0:T(8,128)(2,1)} copy(bf16[16,8,240,128]{3,2,1,0:T(8,128)(2,1)} %bitcast.29) | data formatting | bytes 15728640
  232.4 10.6 %copy.39 = bf16[30720,128]{1,0:T(8,128)(2,1)} copy(bf16[30720,128]{0,1:T(8,128)(2,1)} %bitcast.71) | data formatting | bytes 15728640 | tf_op jit(solution)/shard_map/dot_general | solution.py:74
  243.0 8.3 %multiply_reduce_fusion = f32[192,30,128]{2,0,1:T(8,128)} fusion(f32[192,8,128]{2,0,1:T(8,128)S(1)} %bitcast.86, bf16[8,30,128,128]{3,2,1,0:T(8,128)(2,1)} %bitcast.75, s32[128]{0:T(128)S(1)} %eq.47), kind=kOutput, calls=%fused_computation.7 | convolution fusion | flops 1521033216 | bytes 11600384 | tf_op jit(solution)/shard_map/dot_general | solution.py:74
  251.4 2.3 pad.4
  253.7 3.5 copy.46
  257.2 0.0 copy-start.7
  257.2 0.0 all-reduce.3.cloned.1.call-update
  257.2 0.7 copy-done.7
  257.9 0.2 copy-done.4
  258.1 0.0 copy-done.8
  258.2 0.1 reshape.171
  258.3 25.8 %all-reduce.3.cloned.1.call-done = f32[30,24576]{1,0:T(8,128)} async-done(((f32[30,24576]{1,0:T(8,128)}), f32[30,24576]{1,0:T(8,128)}) %all-reduce.3.cloned.1.call-update) | async-done | bytes 2949136 | tf_op jit(solution)/shard_map/psum | solution.py:81
  284.1 12.3 %convert_reduce_fusion = (f32[30,24576]{1,0:T(8,128)S(1)}, f32[10,24576]{1,0:T(8,128)}) fusion(bf16[10,30,24576]{2,1,0:T(8,128)(2,1)} %param.11, f32[30,24576]{1,0:T(8,128)} %all-reduce.3.cloned.1.call-done), kind=kLoop, calls=%fused_computation.4 | loop fusion | flops 28508160 | bytes 21626880 | tf_op jit(solution)/shard_map/reduce_sum | solution.py:61
  296.4 2.0 broadcast_multiply_fusion
  298.3 12.6 %all-reduce.4 = bf16[30,24576]{1,0:T(8,128)(2,1)} all-reduce(f32[30,24576]{1,0:T(8,128)} %broadcast_multiply_fusion), channel_id=1, replica_groups=mesh['tiles'=16,'lev'=2] {'lev'}, use_global_device_ids=true, to_apply=%region_9.10 | all-reduce | flops 737280 | bytes 4423680 | tf_op jit(solution)/shard_map/psum | solution.py:62
  310.9 1.8 copy.47
  312.7 0.1 slice.8
  312.8 2.1 copy.55
  314.9 2.2 gather_fusion.2
  317.0 1.2 broadcast_select_fusion
  318.2 6.5 %all-to-all-start.2 = ((bf16[128,30,128]{2,1,0:T(8,128)(2,1)}), bf16[128,30,128]{2,1,0:T(8,128)(2,1)S(1)}, u32[]{:S(2)}, u32[]{:S(2)}) async-start(bf16[128,30,128]{2,1,0:T(8,128)(2,1)} %broadcast_select_fusion), calls=%async_computation.2 | async-start | bytes 2097152 | tf_op jit(solution)/shard_map/all_to_all | solution.py:84
  324.8 2.4 multiply_reduce_fusion.2
  327.2 0.0 copy-done.5
  327.2 0.0 copy-done.2
  327.2 1.6 multiply_multiply_fusion
  328.9 20.7 %all-to-all-done.2 = bf16[128,30,128]{2,1,0:T(8,128)(2,1)S(1)} async-done(((bf16[128,30,128]{2,1,0:T(8,128)(2,1)}), bf16[128,30,128]{2,1,0:T(8,128)(2,1)S(1)}, u32[]{:S(2)}, u32[]{:S(2)}) %all-to-all-start.2) | async-done | bytes 983072 | tf_op jit(solution)/shard_map/all_to_all | solution.py:84
  349.5 1.4 gather_fusion.3
  350.9 2.4 bitcast_reduce_fusion
  353.4 0.0 copy-start.6
  353.4 0.1 multiply_reduce_fusion.3
  353.5 0.3 copy.42
  353.8 0.3 copy.48
  354.1 0.0 copy-done.1
  354.2 0.4 multiply_reduce_fusion.1
  354.6 0.0 copy-done.6
  354.6 0.8 multiply_multiply_fusion.1
  (20 shorter events, 0.2 us)
Async XLA Ops:
  7.2 15.2 %copy-start = (bf16[64,128,128]{2,1,0:T(8,128)(2,1)S(1)}, bf16[64,128,128]{2,1,0:T(8,128)(2,1)}, u32[]{:S(2)}) copy-start(bf16[64,128,128]{2,1,0:T(8,128)(2,1)} %param.12) | copy-start | bytes 6291460
  12.1 30.2 %all-to-all-start = ((s32[16,8,1]{1,2,0:T(1,128)}), s32[16,8,1]{1,2,0:T(1,128)S(1)}, u32[]{:S(2)}, u32[]{:S(2)}) async-start(s32[16,8,1]{1,2,0:T(1,128)} %bitcast.3), calls=%async_computation | async-start | bytes 16384 | tf_op jit(solution)/shard_map/all_to_all | solution.py:69
  42.3 6.7 %copy-start.3 = (bf16[8,24576]{1,0:T(8,128)(2,1)S(1)}, bf16[8,24576]{1,0:T(8,128)(2,1)}, u32[]{:S(2)}) copy-start(bf16[8,24576]{1,0:T(8,128)(2,1)} %param.15) | copy-start | bytes 1179652
  42.3 181.7 %all-to-all-start.1 = ((bf16[128,240,128]{2,1,0:T(8,128)(2,1)}), bf16[128,240,128]{2,1,0:T(8,128)(2,1)}, u32[]{:S(2)}, u32[]{:S(2)}) async-start(bf16[128,240,128]{2,1,0:T(8,128)(2,1)} %select_multiply_fusion), calls=%async_computation.1 | async-start | bytes 15728640 | tf_op jit(solution)/shard_map/all_to_all | solution.py:68
  48.8 235.3 %all-reduce.3.cloned.1.call-start = ((), (), s32[]{:S(2)}) async-start(), calls=%async_computation.3 | async-start | bytes 6291456 | tf_op jit(solution)/shard_map/psum | solution.py:81
  257.2 0.7 copy-start.7
  257.2 0.9 copy-start.4
  257.2 0.9 copy-start.8
  318.2 9.0 %copy-start.5 = (f32[24576]{0:T(1024)S(1)}, f32[24576]{0:T(1024)}, u32[]{:S(2)}) copy-start(f32[24576]{0:T(1024)} %param.16) | copy-start | bytes 294916
  318.2 31.3 %all-to-all-start.2 = ((bf16[128,30,128]{2,1,0:T(8,128)(2,1)}), bf16[128,30,128]{2,1,0:T(8,128)(2,1)S(1)}, u32[]{:S(2)}, u32[]{:S(2)}) async-start(bf16[128,30,128]{2,1,0:T(8,128)(2,1)} %broadcast_select_fusion), calls=%async_computation.2 | async-start | bytes 2097152 | tf_op jit(solution)/shard_map/all_to_all | solution.py:84
  324.8 2.5 copy-start.2
  350.9 3.2 copy-start.1
  353.4 1.2 copy-start.6
Sparse Core Ops, SparseCore 0:
  257.3 26.6 all-reduce.2
where the time goes:
time: 365 us; the launch traced here: 362 us
  waiting for transfers between devices  220 us (60%)
  local copies, waits for them, and re-layouts  49.3 us (14%)
  other arithmetic  31.4 us (9%)
  starting transfers between devices  19.9 us (5%)
  matrix products  14.9 us (4%)
  between operations  14.3 us (4%)
  blocking collectives  12.6 us (3%)
    all_to_all x1, waiting for transfers between devices, shards(): lax.all_to_all(sent, 'tiles', split_axis=0, concat_axis=0, tiled=True)  173 us
    psum x1, waiting for transfers between devices, shards(): proj = lax.psum(proj_part, 'lev')  25.8 us
    all_to_all x1, waiting for transfers between devices, shards(): lax.all_to_all(answer, 'tiles', split_axis=0, concat_axis=0, tiled=True)  20.7 us
    unnamed x25, local copies, waits for them, and re-layouts  19.2 us
    psum x1, blocking collectives, shards(): layer_mean = lax.psum(layer_part, 'lev')  12.6 us
    reduce_sum x1, other arithmetic, shards(): layer_part = jnp.sum(ocn_anom.astype(jnp.float32), axis=0) / OLEV  12.3 us
    dot_general x1, local copies, waits for them, and re-layouts, shards(): jnp.dot(owner_hot, arrived.reshape(slots, rows * 128), preferred_element_...  10.6 us
    gather x1, local copies, waits for them, and re-layouts, shards(): sent = jnp.take(remapped, slot_src, axis=0) * keep  8.6 us
  transfers between devices with their start and end apart: 4, of which 3 were waited for; matrix products, arithmetic and copies ran while one was open for 8% of the time, Pallas kernels for 0%

commit v1 on v0

v1 whole, which is shorter than its diff:
```python
import functools

import jax
import jax.numpy as jnp
from jax import lax
from jax.experimental import pallas as pl
from jax.experimental.pallas import tpu as pltpu
from jax.sharding import PartitionSpec as P

MEM = 30
HALF = 16
OLEV = 20
LTAP = 8
MESH = pl.DeviceIdType.MESH
VLIM = 56 * 1024 * 1024


def layer_kernel(x_ref, out_ref):
    total = x_ref[0].astype(jnp.float32)
    for level in range(1, x_ref.shape[0]):
        total = total + x_ref[level].astype(jnp.float32)
    out_ref[0] = total[:HALF]
    out_ref[1, : MEM - HALF, :] = total[HALF:]
    out_ref[1, MEM - HALF :, :] = jnp.zeros((2 * HALF - MEM, total.shape[1]), jnp.float32)


def layer_parts(ocn_anom, chunk):
    lev, mem, cells = ocn_anom.shape
    return pl.pallas_call(
        layer_kernel,
        grid=(cells // chunk,),
        in_specs=[pl.BlockSpec((lev, mem, chunk), lambda i: (0, 0, i))],
        out_specs=pl.BlockSpec((2, HALF, chunk), lambda i: (0, 0, i)),
        out_shape=jax.ShapeDtypeStruct((2, HALF, cells), jnp.float32),
        compiler_params=pltpu.CompilerParams(vmem_limit_bytes=VLIM),
        cost_estimate=pl.CostEstimate(
            flops=lev * mem * cells, bytes_accessed=2 * lev * mem * cells, transcendentals=0
        ),
    )(ocn_anom)


def greet(nt, me, lev):
    barrier = pltpu.get_barrier_semaphore()

    def signal(k, carry):
        pl.semaphore_signal(
            barrier, inc=1, device_id=(lax.rem(me + k, nt), lev), device_id_type=MESH
        )
        return carry

    lax.fori_loop(1, nt, signal, 0)
    pl.semaphore_signal(barrier, inc=1, device_id=(me, 1 - lev), device_id_type=MESH)
    pl.semaphore_wait(barrier, nt)


def answer_kernel(
    nt, per, part_ref, idx_ref, obs_ref,
    lay_ref, w_ref, blk_ref,
    peer, layer, obs, lay_out, w_out, blk_smem,
    peer_sems, smem_sem, idx_send, idx_recv, w_send, w_recv, lay_send, lay_recv,
):
    me, lev = lax.axis_index("tiles"), lax.axis_index("lev")
    oblk = layer.shape[0]
    greet(nt, me, lev)
    swap = pltpu.make_async_remote_copy(
        src_ref=part_ref.at[1 - lev], dst_ref=peer, send_sem=peer_sems.at[0],
        recv_sem=peer_sems.at[1], device_id=(me, 1 - lev), device_id_type=MESH,
    )
    swap.start()

    def move(src, dst, send, recv, k):
        to = lax.rem(me + k, nt)
        return pltpu.make_async_remote_copy(
            src_ref=src.at[to], dst_ref=dst.at[me], send_sem=send.at[k], recv_sem=recv.at[k],
            device_id=(to, lev), device_id_type=MESH,
        )

    def arrival(src, dst, send, recv, k):
        frm = lax.rem(me + nt - k, nt)
        return pltpu.make_async_remote_copy(
            src_ref=src.at[frm], dst_ref=dst.at[frm], send_sem=send.at[k], recv_sem=recv.at[k],
            device_id=(frm, lev), device_id_type=MESH,
        )

    idx_set = (idx_ref, blk_ref, idx_send, idx_recv)
    w_set = (w_out, w_ref, w_send, w_recv)
    lay_set = (lay_out, lay_ref, lay_send, lay_recv)

    def each(fn):
        def body(k, carry):
            fn(k)
            return carry

        lax.fori_loop(1, nt, body, 0)

    each(lambda k: move(*idx_set, k).start())

    def lanes(o):
        return pl.ds(pl.multiple_of(o * 128, 128), 128)

    def widen(o, carry):
        obs[o] = obs_ref[:, lanes(o)].astype(jnp.float32)
        return carry

    lax.fori_loop(0, oblk, widen, 0)
    blk_ref[me] = idx_ref[me]
    each(lambda k: arrival(*idx_set, k).wait_recv())
    each(lambda k: move(*idx_set, k).wait_send())
    down = pltpu.make_async_copy(blk_ref, blk_smem, smem_sem)
    down.start()
    down.wait()

    def fill_w(to, dst):
        for s in range(0, per, 2):
            pair = [obs[blk_smem[to, s + j, 0]] for j in range(2)]
            dst[to, 8 * s : 8 * s + 16, :] = jnp.concatenate(pair, axis=0).astype(jnp.bfloat16)

    def fill_lay(to, dst):
        for s in range(per):
            dst[to, HALF * s : HALF * (s + 1), :] = layer[blk_smem[to, s, 0]]

    def send_w(k):
        fill_w(lax.rem(me + k, nt), w_out)
        move(*w_set, k).start()

    each(send_w)
    fill_w(me, w_ref)
    swap.wait()

    def mean(o, carry):
        at = lanes(o)
        layer[o] = ((part_ref[lev, :, at] + peer[:, at]) / OLEV).astype(jnp.bfloat16)
        return carry

    lax.fori_loop(0, oblk, mean, 0)

    def send_lay(k):
        fill_lay(lax.rem(me + k, nt), lay_out)
        move(*lay_set, k).start()

    each(send_lay)
    fill_lay(me, lay_ref)
    each(lambda k: arrival(*w_set, k).wait_recv())
    each(lambda k: arrival(*lay_set, k).wait_recv())
    each(lambda k: move(*w_set, k).wait_send())
    each(lambda k: move(*lay_set, k).wait_send())


def answers(part, idx, obs, nt, per):
    cells = part.shape[2]
    vmem = pl.BlockSpec(memory_space=pltpu.VMEM)
    dma = pltpu.SemaphoreType.DMA
    return pl.pallas_call(
        functools.partial(answer_kernel, nt, per),
        out_shape=(
            jax.ShapeDtypeStruct((nt, per * HALF, 128), jnp.bfloat16),
            jax.ShapeDtypeStruct((nt, per * 8, 128), jnp.bfloat16),
            jax.ShapeDtypeStruct((nt, 8, 128), jnp.int32),
        ),
        in_specs=[vmem] * 3,
        out_specs=(vmem,) * 3,
        scratch_shapes=[
            pltpu.VMEM((HALF, cells), jnp.float32),
            pltpu.VMEM((cells // 128, HALF, 128), jnp.bfloat16),
            pltpu.VMEM((cells // 128, 8, 128), jnp.float32),
            pltpu.VMEM((nt, per * HALF, 128), jnp.bfloat16),
            pltpu.VMEM((nt, per * 8, 128), jnp.bfloat16),
            pltpu.SMEM((nt, 8, 128), jnp.int32),
            dma((2,)),
            dma,
        ]
        + [dma((nt,))] * 6,
        compiler_params=pltpu.CompilerParams(
            collective_id=0, has_side_effects=True, vmem_limit_bytes=VLIM
        ),
    )(part, idx, obs)


def remap_kernel(group, rpb, slot_ref, x_ref, w_ref, lay_ref, obs_ref, con_ref, oa_ref, xs):
    lev = x_ref.shape[0]
    i = pl.program_id(0)

    @pl.when(i == 0)
    def _():
        xs[...] = jnp.zeros_like(xs)

    xs[:, :MEM, :] = x_ref[...]
    for j in range(group):
        weights = jnp.concatenate([w_ref[j * rpb + r] for r in range(rpb)], axis=1)
        x = xs[:, :, 128 * j : 128 * (j + 1)].reshape(lev * 2 * HALF, 128)
        y = jnp.dot(x, weights, preferred_element_type=jnp.float32)
        y = y.astype(jnp.bfloat16).astype(jnp.float32).reshape(lev, 2 * HALF, rpb * 128)
        obs, lay = [], []
        for r in range(rpb):
            slot = slot_ref[(i * group + j) * rpb + r]
            pair = obs_ref[pl.ds(pl.multiple_of((slot // 2) * 16, 16), 16), :].astype(jnp.float32)
            obs.append(jnp.where(slot % 2 == 0, pair[:8], pair[8:]))
            lay.append(lay_ref[pl.ds(pl.multiple_of(slot * HALF, HALF), HALF), :])
        obs = jnp.concatenate(obs, axis=1)
        total = y[0] * obs[0:1]
        for level in range(1, lev):
            total = total + y[level] * obs[level : level + 1]
        for r in range(rpb):
            for h in range(2):
                con_ref[h, j * rpb + r] = total[h * HALF : (h + 1) * HALF, 128 * r : 128 * (r + 1)]
        oa_ref[:, 128 * j : 128 * (j + 1)] = lax.dot_general(
            jnp.concatenate(lay, axis=1), weights, (((1,), (1,)), ((), ())),
            preferred_element_type=jnp.float32,
        )


def remap(slot_of, atm_anom, remap_w, lay, obs, group):
    lev, mem, cells = atm_anom.shape
    ablk, nrem = cells // 128, remap_w.shape[0]
    rpb = nrem // ablk
    lay, obs = lay.reshape(-1, 128), obs.reshape(-1, 128)
    return pl.pallas_call(
        functools.partial(remap_kernel, group, rpb),
        grid_spec=pltpu.PrefetchScalarGridSpec(
            num_scalar_prefetch=1,
            grid=(ablk // group,),
            in_specs=[
                pl.BlockSpec((lev, mem, 128 * group), lambda i, s: (0, 0, i)),
                pl.BlockSpec((rpb * group, 128, 128), lambda i, s: (i, 0, 0)),
                pl.BlockSpec(lay.shape, lambda i, s: (0, 0)),
                pl.BlockSpec(obs.shape, lambda i, s: (0, 0)),
            ],
            out_specs=[
                pl.BlockSpec((2, rpb * group, HALF, 128), lambda i, s: (0, i, 0, 0)),
                pl.BlockSpec((HALF, 128 * group), lambda i, s: (0, i)),
            ],
            scratch_shapes=[pltpu.VMEM((lev, 2 * HALF, 128 * group), jnp.bfloat16)],
        ),
        out_shape=[
            jax.ShapeDtypeStruct((2, nrem, HALF, 128), jnp.float32),
            jax.ShapeDtypeStruct((HALF, cells), jnp.float32),
        ],
        compiler_params=pltpu.CompilerParams(vmem_limit_bytes=VLIM),
        cost_estimate=pl.CostEstimate(
            flops=2 * nrem * lev * 32 * 128 * 128, bytes_accessed=8 << 20, transcendentals=0
        ),
    )(slot_of, atm_anom, remap_w, lay, obs)


def return_kernel(
    nt, per, src_ref, con_ref, oa_ref,
    got_ref, oa_out,
    peer, summed, out, peer_sems, oa_sems, send, recv, fsend, frecv,
):
    me, lev = lax.axis_index("tiles"), lax.axis_index("lev")
    greet(nt, me, lev)
    partner = (me, 1 - lev)
    swap = pltpu.make_async_remote_copy(
        src_ref=con_ref.at[1 - lev], dst_ref=peer, send_sem=peer_sems.at[0],
        recv_sem=peer_sems.at[1], device_id=partner, device_id_type=MESH,
    )
    swap.start()
    oa_swap = pltpu.make_async_remote_copy(
        src_ref=oa_ref, dst_ref=oa_out.at[lev], send_sem=oa_sems.at[0],
        recv_sem=oa_sems.at[1], device_id=partner, device_id_type=MESH,
    )
    oa_swap.start()
    oa_out[lev] = oa_ref[...]
    swap.wait()

    def add(i, carry):
        at = pl.ds(i * 8, 8)
        summed[at] = (con_ref[lev, at] + peer[at]).astype(jnp.bfloat16)
        return carry

    lax.fori_loop(0, con_ref.shape[1] // 8, add, 0)

    def move(k):
        to = lax.rem(me + k, nt)
        return pltpu.make_async_remote_copy(
            src_ref=out.at[to], dst_ref=got_ref.at[lev, me], send_sem=send.at[k],
            recv_sem=recv.at[k], device_id=(to, lev), device_id_type=MESH,
        )

    def arrival(k):
        frm = lax.rem(me + nt - k, nt)
        return pltpu.make_async_remote_copy(
            src_ref=out.at[frm], dst_ref=got_ref.at[lev, frm], send_sem=send.at[k],
            recv_sem=recv.at[k], device_id=(frm, lev), device_id_type=MESH,
        )

    def forward(k, half):
        frm = lax.rem(me + nt - k, nt)
        return pltpu.make_async_remote_copy(
            src_ref=got_ref.at[half, frm], dst_ref=got_ref.at[half, frm], send_sem=fsend.at[k],
            recv_sem=frecv.at[k], device_id=partner, device_id_type=MESH,
        )

    def start(k, carry):
        to = lax.rem(me + k, nt)
        for s in range(per):
            out[to, s * HALF : (s + 1) * HALF, :] = summed[src_ref[to * per + s]]
        move(k).start()
        return carry

    lax.fori_loop(1, nt, start, 0)
    for s in range(per):
        got_ref[lev, me, s * HALF : (s + 1) * HALF, :] = summed[src_ref[me * per + s]]
    forward(0, lev).start()

    def pass_on(k, carry):
        arrival(k).wait_recv()
        forward(k, lev).start()
        return carry

    lax.fori_loop(1, nt, pass_on, 0)

    def finish(k, carry):
        forward(k, 1 - lev).wait_recv()
        forward(k, lev).wait_send()
        return carry

    lax.fori_loop(0, nt, finish, 0)

    def sent(k, carry):
        move(k).wait_send()
        return carry

    lax.fori_loop(1, nt, sent, 0)
    oa_swap.wait()


def give_back(slot_src, con, oa, nt, per):
    nrem = con.shape[1]
    vmem = pl.BlockSpec(memory_space=pltpu.VMEM)
    dma = pltpu.SemaphoreType.DMA
    return pl.pallas_call(
        functools.partial(return_kernel, nt, per),
        out_shape=(
            jax.ShapeDtypeStruct((2, nt, per * HALF, 128), jnp.bfloat16),
            jax.ShapeDtypeStruct((2,) + oa.shape, jnp.float32),
        ),
        in_specs=[pl.BlockSpec(memory_space=pltpu.SMEM), vmem, vmem],
        out_specs=(vmem, vmem),
        scratch_shapes=[
            pltpu.VMEM((nrem, HALF, 128), jnp.float32),
            pltpu.VMEM((nrem, HALF, 128), jnp.bfloat16),
            pltpu.VMEM((nt, per * HALF, 128), jnp.bfloat16),
            dma((2,)),
            dma((2,)),
        ]
        + [dma((nt,))] * 4,
        compiler_params=pltpu.CompilerParams(
            collective_id=1, has_side_effects=True, vmem_limit_bytes=VLIM
        ),
    )(slot_src, con, oa)


def increment_kernel(slots, blk_ref, got_ref, x_ref, innov_ref, band_ref, out_ref, proj):
    i = pl.program_id(0)
    lev, mem, chunk = x_ref.shape
    first = lax.axis_index("lev") * lev

    @pl.when(i == 0)
    def _():
        proj[...] = jnp.zeros_like(proj)

        def put(s, carry):
            blk = blk_ref[s]

            @pl.when(blk >= 0)
            def _():
                at = pl.ds(pl.multiple_of(blk * 128, 128), 128)
                for h in range(2):
                    proj[h * HALF : (h + 1) * HALF, at] += got_ref[h, s].astype(jnp.float32)

            return carry

        lax.fori_loop(0, slots, put, 0)

    at = pl.ds(pl.multiple_of(i * chunk, chunk), chunk)
    p = proj[:, at]
    var = jnp.sum(p * p, axis=0, keepdims=True) / (MEM - 1) + 0.1
    scale = innov_ref[...] / var / (MEM - 1)
    band = band_ref[...].astype(jnp.float32)
    p = p[:mem]
    for level in range(lev):
        cov = jnp.sum(x_ref[level].astype(jnp.float32) * p, axis=0, keepdims=True)
        dist = jnp.abs((first + level).astype(jnp.float32) - band)
        taper = jnp.maximum(0.0, 1.0 - dist / LTAP)
        out_ref[level : level + 1, :] = taper * cov * scale


def ocean_increment(blk, got, ocn_anom, innov, band, chunk):
    lev, mem, cells = ocn_anom.shape
    slots = got.shape[1]
    return pl.pallas_call(
        functools.partial(increment_kernel, slots),
        grid_spec=pltpu.PrefetchScalarGridSpec(
            num_scalar_prefetch=1,
            grid=(cells // chunk,),
            in_specs=[
                pl.BlockSpec(got.shape, lambda i, s: (0, 0, 0, 0)),
                pl.BlockSpec((lev, mem, chunk), lambda i, s: (0, 0, i)),
                pl.BlockSpec((1, chunk), lambda i, s: (0, i)),
                pl.BlockSpec((1, chunk), lambda i, s: (0, i)),
            ],
            out_specs=pl.BlockSpec((lev, chunk), lambda i, s: (0, i)),
            scratch_shapes=[pltpu.VMEM((2 * HALF, cells), jnp.float32)],
        ),
        out_shape=jax.ShapeDtypeStruct((lev, cells), jnp.float32),
        compiler_params=pltpu.CompilerParams(vmem_limit_bytes=VLIM),
        cost_estimate=pl.CostEstimate(
            flops=2 * lev * mem * cells, bytes_accessed=2 * lev * mem * cells, transcendentals=0
        ),
    )(blk, got, ocn_anom, innov.reshape(1, -1), band.reshape(1, -1))


def taper_levels(first, levels, band):
    lvl = (first + jnp.arange(levels, dtype=jnp.int32)).astype(jnp.float32)[:, None]
    return jnp.maximum(0.0, 1.0 - jnp.abs(lvl - band[None, :].astype(jnp.float32)) / LTAP)


def increment(anom, proj, tapered, innov):
    cov = jnp.sum(anom.astype(jnp.float32) * proj[None], axis=1) / (MEM - 1)
    var = jnp.sum(proj * proj, axis=0) / (MEM - 1) + 0.1
    return tapered * cov * (innov / var)[None, :]


def shards(
    atm_anom,
    ocn_anom,
    remap_w,
    rem_tile,
    rem_block,
    obs_weight,
    innov_ocn,
    innov_atm,
    band_ocn,
    band_atm,
):
    nt = lax.axis_size("tiles")
    lev = lax.axis_index("lev")
    alev, _, acells = atm_anom.shape
    nrem = remap_w.shape[0]
    per = max(2, 2 * ((nrem + nt - 1) // nt))
    slots = nt * per
    dest = rem_tile[:, 0]
    match_dest = (dest[:, None] == jnp.arange(nt, dtype=jnp.int32)[None, :]).astype(jnp.int32)
    rank = jnp.sum(jnp.cumsum(match_dest, axis=0) * match_dest, axis=1) - 1
    slot_of = dest * per + rank
    match_slot = (slot_of[None, :] == jnp.arange(slots, dtype=jnp.int32)[:, None]).astype(jnp.int32)
    slot_src = jnp.sum(match_slot * jnp.arange(nrem, dtype=jnp.int32)[None, :], axis=1)
    send_blk = jnp.sum(match_slot * (rem_block + 1)[None, :], axis=1) - 1
    idx = jnp.broadcast_to(send_blk.reshape(nt, per, 1), (nt, per, 128))
    idx = jnp.where(jnp.arange(128) == 0, jnp.maximum(idx, 0), idx)
    idx = jnp.pad(idx, ((0, 0), (0, 8 - per), (0, 0)))
    part = layer_parts(ocn_anom, 2048)
    lay, obs, blk = answers(part, idx, obs_weight, nt, per)
    con, oa = remap(slot_of, atm_anom, remap_w, lay, obs, 4)
    got, oa2 = give_back(slot_src, con, oa, nt, per)
    blk = blk[:, :per, 1].reshape(slots)
    got = got.reshape(2, slots, HALF, 128)
    ocn_increment = ocean_increment(blk, got, ocn_anom, innov_ocn, band_ocn, 2048)
    ocn_on_atm = oa2.reshape(2 * HALF, acells)[:MEM]
    taper_atm = taper_levels(lev * alev, alev, band_atm)
    atm_increment = increment(atm_anom, ocn_on_atm, taper_atm, innov_atm)
    return (ocn_increment, atm_increment)


def solution(mesh):
    in_specs = (
        P("lev", None, "tiles"),
        P("lev", None, "tiles"),
        P("tiles", None, None),
        P("tiles", None),
        P("tiles"),
        P("lev", "tiles"),
        P("tiles"),
        P("tiles"),
        P("tiles"),
        P("tiles"),
    )
    out_specs = (P("lev", "tiles"), P("lev", "tiles"))
    return jax.shard_map(shards, mesh=mesh, in_specs=in_specs, out_specs=out_specs, check_vma=False)
```

time: 365 us -> 99.3 us (0.27)
  waiting for transfers between devices: 220 us -> 0 us
  Pallas kernels: 0 us -> 89.9 us
  local copies, waits for them, and re-layouts: 49.3 us -> 4.58 us
  other arithmetic: 31.4 us -> 3.01 us
  starting transfers between devices: 19.9 us -> 0 us
  matrix products: 14.9 us -> 0 us
  between operations: 14.3 us -> 0.76 us
  blocking collectives: 12.6 us -> 0 us
    all_to_all x3 -> x0, waiting for transfers between devices: 194 us -> none  [the longest x1 173 us: shards(): lax.all_to_all(sent, 'tiles', split_axis=0, concat_axis=0, tiled=True)]
    pallas_call x0 -> x5, Pallas kernels: none -> 89.9 us  [the longest x1 30.4 us: answers(): pl.pallas_call(functools.partial(answer_kernel, nt, per), out_shape=(jax....]
    psum x1 -> x0, waiting for transfers between devices: 25.8 us -> none  [shards(): proj = lax.psum(proj_part, 'lev')]
    all_to_all x3 -> x0, starting transfers between devices: 19.6 us -> none  [the longest x1 6.61 us: shards(): lax.all_to_all(send_blk, 'tiles', split_axis=0, concat_axis=0, tiled=True)]
    unnamed x25 -> x15, local copies, waits for them, and re-layouts: 19.2 us -> 2.63 us
    dot_general x3 -> x0, matrix products: 14.9 us -> none  [the longest x1 8.35 us: shards(): jnp.dot(owner_hot, arrived.reshape(slots, rows * 128), preferred_element_...]
    gather x4 -> x0, local copies, waits for them, and re-layouts: 13.8 us -> none  [the longest x1 8.6 us: shards(): sent = jnp.take(remapped, slot_src, axis=0) * keep]
    psum x1 -> x0, blocking collectives: 12.6 us -> none  [shards(): layer_mean = lax.psum(layer_part, 'lev')]
  transfers between devices with their start and end apart: 4 -> 0, of which waited for: 3 -> 0; matrix products, arithmetic and copies ran while one was open for 8% -> 0% of each run, Pallas kernels for 0% -> 0%
where the time goes in v1:
time: 99.3 us; the launch traced here: 98.2 us
  Pallas kernels  89.9 us (91%)
  local copies, waits for them, and re-layouts  4.58 us (5%)
  other arithmetic  3.01 us (3%)
    pallas_call x1, Pallas kernels, answers(): pl.pallas_call(functools.partial(answer_kernel, nt, per), out_shape=(jax....  30.4 us
    pallas_call x1, Pallas kernels, give_back(): pl.pallas_call(functools.partial(return_kernel, nt, per), out_shape=(jax....  24 us
    pallas_call x1, Pallas kernels, ocean_increment(): pl.pallas_call(functools.partial(increment_kernel, slots), grid_spec=pltp...  16.1 us
    pallas_call x1, Pallas kernels, layer_parts(): pl.pallas_call(layer_kernel, grid=(cells // chunk,), in_specs=[pl.BlockSp...  11.3 us
    pallas_call x1, Pallas kernels, remap(): pl.pallas_call(functools.partial(remap_kernel, group, rpb), grid_spec=plt...  8.06 us
    unnamed x15, local copies, waits for them, and re-layouts  2.63 us

profile of v1, /device:TPU:13, one launch (start us, length us, event | category | flops | bytes accessed | tf_op | source)
XLA Modules:
  0.0 98.2 jit_solution(11740449034210214028)
XLA Ops:
  0.6 0.0 copy-start.4
  0.6 0.0 copy-start.6
  0.6 11.3 %shard_map.113.part_ref = f32[2,16,24576]{2,1,0:T(8,128)} custom-call(bf16[10,30,24576]{2,1,0:T(8,128)(2,1)} %x_ref.4), custom_call_target="tpu_custom_call" | custom-call | flops 7372800 | bytes 14745600 | tf_op jit(solution)/shard_map/pallas_call | solution.py:29
  11.9 0.0 copy-start
  11.9 0.0 copy-done.4
  11.9 0.1 fusion
  12.0 0.1 reduce_window_sum.11
  12.1 0.2 select_reduce_fusion.2
  12.3 0.0 copy-done.6
  12.3 0.0 copy-start.5
  12.3 0.6 select_reduce_fusion
  12.9 0.1 sub.30
  13.0 0.7 broadcast_select_fusion.idx_ref
  13.8 30.4 %shard_map.114 = (bf16[16,128,128]{2,1,0:T(8,128)(2,1)}, bf16[16,64,128]{2,1,0:T(8,128)(2,1)}, s32[16,8,128]{2,1,0:T(8,128)}) custom-call(f32[2,16,24576]{2,1,0:T(8,128)} %shard_map.113.part_ref, s32[16,8,128]{2,1,0:T(8,128)} %broadcast_select_fusion.idx_ref, bf16[8,24576]{1,0:T(8,128)(2,1)} %obs_ref.1), custom_call_target="tpu_custom_call" | custom-call | tf_op jit(solution)/shard_map/pallas_call | solution.py:153
  44.2 1.3 %slice_reduce_fusion = s32[16,8]{1,0:T(8,128)S(1)} fusion(s32[16,8,128]{2,1,0:T(8,128)} %get-tuple-element.9), kind=kLoop, calls=%fused_computation.3 | loop fusion | bytes 1024 | tf_op jit(solution)/shard_map/slice | solution.py:457
  45.4 0.6 reshape_squeeze.3.blk_ref
  46.1 0.0 copy-done
  46.1 2.4 %copy.14.x_ref = bf16[8,30,4096]{2,1,0:T(8,128)(2,1)} copy(bf16[8,30,4096]{2,0,1:T(8,128)(2,1)S(1)} %copy-done) | data formatting | bytes 3932160 | tf_op args[0]
  48.5 0.0 copy-done.5
  48.5 8.1 %shard_map.115 = (f32[2,64,16,128]{3,2,1,0:T(8,128)}, f32[16,4096]{1,0:T(8,128)}) custom-call(s32[64]{0:T(128)} %copy-done.5, bf16[8,30,4096]{2,1,0:T(8,128)(2,1)} %copy.14.x_ref, bf16[64,128,128]{2,1,0:T(8,128)(2,1)} %w_ref.1, bf16[2048,128]{1,0:T(8,128)(2,1)} %bitcast.9, bf16[1024,128]{1,0:T(8,128)(2,1)} %bitcast.11), custom_call_target="tpu_custom_call" | custom-call | flops 536870912 | bytes 8388608 | tf_op jit(solution)/shard_map/pallas_call | solution.py:217
  56.6 24.0 %shard_map.116 = (bf16[2,16,128,128]{3,2,1,0:T(8,128)(2,1)}, f32[2,16,4096]{2,1,0:T(8,128)}) custom-call(s32[128]{0:T(128)} %get-tuple-element.16.src_ref, f32[2,64,16,128]{3,2,1,0:T(8,128)} %get-tuple-element.12.con_ref, f32[16,4096]{1,0:T(8,128)} %get-tuple-element.13.oa_ref), custom_call_target="tpu_custom_call" | custom-call | tf_op jit(solution)/shard_map/pallas_call | solution.py:332
  80.5 0.0 copy-start.1
  80.5 16.1 %shard_map.117 = f32[10,24576]{1,0:T(8,128)} custom-call(s32[128]{0:T(128)} %reshape_squeeze.3.blk_ref, bf16[2,128,16,128]{3,2,1,0:T(8,128)(2,1)} %bitcast.8, bf16[10,30,24576]{2,1,0:T(8,128)(2,1)} %x_ref.4, f32[1,24576]{1,0:T(1,128)} %bitcast.12, s32[1,24576]{1,0:T(1,128)} %bitcast.13), custom_call_target="tpu_custom_call" | custom-call | flops 14745600 | bytes 14745600 | tf_op jit(solution)/shard_map/pallas_call | solution.py:392
  96.7 0.0 copy-start.2
  96.7 0.0 copy-start.3
  96.7 0.0 copy-done.1
  96.7 0.1 multiply_reduce_fusion.1
  96.8 0.5 multiply_reduce_fusion
  97.2 0.2 copy-done.2
  97.4 0.0 copy-done.3
  97.5 0.8 multiply_multiply_fusion
  (7 shorter events, 0.0 us)
Async XLA Ops:
  0.6 11.3 %copy-start.4 = (s32[64,1]{0,1:T(1,128)S(1)}, s32[64,1]{0,1:T(1,128)}, u32[]{:S(2)}) copy-start(s32[64,1]{0,1:T(1,128)} %param.13) | copy-start | bytes 772
  0.6 11.7 %copy-start.6 = (s32[64]{0:T(128)S(1)}, s32[64]{0:T(128)}, u32[]{:S(2)}) copy-start(s32[64]{0:T(128)} %param.14) | copy-start | bytes 772
  11.9 34.1 %copy-start = (bf16[8,30,4096]{2,0,1:T(8,128)(2,1)S(1)}, bf16[8,30,4096]{2,0,1:T(8,128)(2,1)}, u32[]{:S(2)}) copy-start(bf16[8,30,4096]{2,0,1:T(8,128)(2,1)} %param.10) | copy-start | bytes 5898244
  12.3 36.2 %copy-start.5 = (s32[64]{0:T(128)}, s32[64]{0:T(128)S(1)}, u32[]{:S(2)}) copy-start(s32[64]{0:T(128)S(1)} %get-tuple-element.20.slot_ref) | copy-start | bytes 772
  80.5 16.2 %copy-start.1 = (f32[2,16,4096]{2,1,0:T(8,128)S(1)}, f32[2,16,4096]{2,1,0:T(8,128)}, u32[]{:S(2)}) copy-start(f32[2,16,4096]{2,1,0:T(8,128)} %get-tuple-element.15) | copy-start | bytes 1572868
  96.7 0.7 copy-start.2
  96.7 0.7 copy-start.3

commit v2 on v0

v2 whole, which is shorter than its diff:
```python
import functools

import jax
import jax.numpy as jnp
from jax import lax
from jax.experimental import pallas as pl
from jax.experimental.pallas import tpu as pltpu
from jax.sharding import PartitionSpec as P

MEM = 30
HALF = 16
OLEV = 20
LTAP = 8
MESH = pl.DeviceIdType.MESH
VLIM = 56 * 1024 * 1024


def greet(nt, me, lev):
    barrier = pltpu.get_barrier_semaphore()

    def signal(k, carry):
        pl.semaphore_signal(
            barrier, inc=1, device_id=(lax.rem(me + k, nt), lev), device_id_type=MESH
        )
        return carry

    lax.fori_loop(1, nt, signal, 0)
    pl.semaphore_signal(barrier, inc=1, device_id=(me, 1 - lev), device_id_type=MESH)
    pl.semaphore_wait(barrier, nt)


def loop(first, last, fn):
    def body(k, carry):
        fn(k)
        return carry

    lax.fori_loop(first, last, body, 0)


def lanes(o, width=128):
    return pl.ds(pl.multiple_of(o * width, width), width)


def main_kernel(
    nt, per, chunk, parts,
    slot_ref, src_ref, idx_ref, obs_ref, ocn_hbm, atm_hbm, rw_hbm,
    got_ref, oa_ref, blk_ref,
    ocn, atm, rw, part, peer, layer, obs, lay_out, lay_rx, w_out, w_rx, obs_rx,
    xs, con, con_peer, summed, out, blk_smem,
    ocn_sem, atm_sem, rw_sem, smem_sem, swap_s, swap_r, con_s, con_r, oa_sem,
    idx_s, idx_r, w_s, w_r, lay_s, lay_r, out_s, out_r, fwd_s, fwd_r,
):
    me, lev = lax.axis_index("tiles"), lax.axis_index("lev")
    partner = (me, 1 - lev)
    alev = atm.shape[0]
    nrem = rw.shape[0]
    ablk = atm.shape[2] // 128
    rpb = nrem // ablk
    nchunk = ocn_hbm.shape[2] // chunk

    def fetch(i):
        return pltpu.make_async_copy(
            ocn_hbm.at[:, :, lanes(i, chunk)], ocn.at[lax.rem(i, 2)], ocn_sem.at[lax.rem(i, 2)]
        )

    fetch(0).start()
    atm_copy = pltpu.make_async_copy(atm_hbm, atm, atm_sem)
    rw_copy = pltpu.make_async_copy(rw_hbm, rw, rw_sem)
    greet(nt, me, lev)

    def move(src, dst, send, recv, k):
        to = lax.rem(me + k, nt)
        return pltpu.make_async_remote_copy(
            src_ref=src.at[to], dst_ref=dst.at[me], send_sem=send.at[k], recv_sem=recv.at[k],
            device_id=(to, lev), device_id_type=MESH,
        )

    def arrival(src, dst, send, recv, k):
        frm = lax.rem(me + nt - k, nt)
        return pltpu.make_async_remote_copy(
            src_ref=src.at[frm], dst_ref=dst.at[frm], send_sem=send.at[k], recv_sem=recv.at[k],
            device_id=(frm, lev), device_id_type=MESH,
        )

    idx_set = (idx_ref, blk_ref, idx_s, idx_r)
    w_set = (w_out, w_rx, w_s, w_r)
    lay_set = (lay_out, lay_rx, lay_s, lay_r)
    out_set = (out, got_ref.at[lev], out_s, out_r)

    loop(1, nt, lambda k: move(*idx_set, k).start())
    blk_ref[me] = idx_ref[me]

    def swap(i):
        at = lanes(i, chunk)
        return pltpu.make_async_remote_copy(
            src_ref=part.at[1 - lev, :, at], dst_ref=peer.at[:, at], send_sem=swap_s.at[i],
            recv_sem=swap_r.at[i], device_id=partner, device_id_type=MESH,
        )

    def layer_sum(i, more=True):
        if more:
            fetch(i + 1).start()
        fetch(i).wait()
        now = lax.rem(i, 2)
        sub = 256

        def piece(j):
            here = lanes(j, sub)
            at = pl.ds(pl.multiple_of(i * chunk + j * sub, sub), sub)
            total = ocn[now, 0, :, here].astype(jnp.float32)
            for level in range(1, ocn.shape[1]):
                total = total + ocn[now, level, :, here].astype(jnp.float32)
            part[0, :, at] = total[:HALF]
            part[1, : MEM - HALF, at] = total[HALF:]
            part[1, MEM - HALF :, at] = jnp.zeros((2 * HALF - MEM, sub), jnp.float32)

        loop(0, chunk // sub, piece)
        swap(i).start()

    early = nchunk // 3
    loop(0, early, layer_sum)

    def widen(o):
        obs[o] = obs_ref[:, lanes(o)].astype(jnp.float32)

    loop(0, obs.shape[0], widen)
    loop(1, nt, lambda k: arrival(*idx_set, k).wait_recv())
    loop(1, nt, lambda k: move(*idx_set, k).wait_send())
    down = pltpu.make_async_copy(blk_ref, blk_smem, smem_sem)
    down.start()
    down.wait()

    def fill_w(to, dst):
        for s in range(0, per, 2):
            pair = [obs[blk_smem[to, s + j, 0]] for j in range(2)]
            dst[to, 8 * s : 8 * s + 16, :] = jnp.concatenate(pair, axis=0).astype(jnp.bfloat16)

    def fill_lay(to, dst):
        for s in range(per):
            dst[to, HALF * s : HALF * (s + 1), :] = layer[blk_smem[to, s, 0]]

    def send_w(k):
        fill_w(lax.rem(me + k, nt), w_out)
        move(*w_set, k).start()

    loop(1, nt, send_w)
    fill_w(me, w_rx)
    loop(early, nchunk - 1, layer_sum)
    layer_sum(nchunk - 1, False)
    atm_copy.start()
    rw_copy.start()
    xs[...] = jnp.zeros_like(xs)

    def mean(i):
        swap(i).wait()

        def one(j):
            o = i * (chunk // 128) + j
            at = lanes(o)
            layer[o] = ((part[lev, :, at] + peer[:, at]) / OLEV).astype(jnp.bfloat16)

        loop(0, chunk // 128, one)

    loop(0, nchunk, mean)

    def send_lay(k):
        fill_lay(lax.rem(me + k, nt), lay_out)
        move(*lay_set, k).start()

    loop(1, nt, send_lay)
    for s in range(per):
        lay_rx[me, HALF * s : HALF * (s + 1), :] = layer[blk_smem[me, s, 0]]
    atm_copy.wait()
    rw_copy.wait()
    loop(1, nt, lambda k: arrival(*w_set, k).wait_recv())

    def spread(t):
        for s in range(0, per, 2):
            pair = w_rx[t, 8 * s : 8 * s + 16, :].astype(jnp.float32)
            obs_rx[t * per + s] = pair[:8]
            obs_rx[t * per + s + 1] = pair[8:]

    loop(0, nt, spread)

    def weights(b):
        return jnp.concatenate([rw[b * rpb + r] for r in range(rpb)], axis=1)

    def remap(b):
        xs[:, :MEM, :] = atm[:, :, lanes(b)]
        y = jnp.dot(
            xs[...].reshape(alev * 2 * HALF, 128), weights(b), preferred_element_type=jnp.float32
        )
        y = y.astype(jnp.bfloat16).astype(jnp.float32).reshape(alev, 2 * HALF, rpb * 128)
        local = jnp.concatenate([obs_rx[slot_ref[b * rpb + r]] for r in range(rpb)], axis=1)
        total = y[0] * local[0:1]
        for level in range(1, alev):
            total = total + y[level] * local[level : level + 1]
        for r in range(rpb):
            for h in range(2):
                con[h, b * rpb + r] = total[h * HALF : (h + 1) * HALF, 128 * r : 128 * (r + 1)]

    def con_swap(c):
        at = pl.ds(c * (nrem // parts), nrem // parts)
        return pltpu.make_async_remote_copy(
            src_ref=con.at[1 - lev, at], dst_ref=con_peer.at[at], send_sem=con_s.at[c],
            recv_sem=con_r.at[c], device_id=partner, device_id_type=MESH,
        )

    def remap_part(c):
        loop(c * (ablk // parts), (c + 1) * (ablk // parts), remap)
        con_swap(c).start()

    loop(0, parts, remap_part)

    def add(c):
        con_swap(c).wait()

        def four(j):
            at = pl.ds(c * (nrem // parts) + j * 4, 4)
            summed[at] = (con[lev, at] + con_peer[at]).astype(jnp.bfloat16)

        loop(0, nrem // parts // 4, four)

    loop(0, parts, add)

    def send_out(k):
        to = lax.rem(me + k, nt)
        for s in range(per):
            out[to, s * HALF : (s + 1) * HALF, :] = summed[src_ref[to * per + s]]
        move(*out_set, k).start()

    loop(1, nt, send_out)
    for s in range(per):
        got_ref[lev, me, s * HALF : (s + 1) * HALF, :] = summed[src_ref[me * per + s]]

    def forward(k, half):
        frm = lax.rem(me + nt - k, nt)
        return pltpu.make_async_remote_copy(
            src_ref=got_ref.at[half, frm], dst_ref=got_ref.at[half, frm], send_sem=fwd_s.at[k],
            recv_sem=fwd_r.at[k], device_id=partner, device_id_type=MESH,
        )

    forward(0, lev).start()
    loop(1, nt, lambda k: arrival(*lay_set, k).wait_recv())

    def split(t):
        for s in range(per):
            layer[t * per + s] = lay_rx[t, HALF * s : HALF * (s + 1), :]

    loop(1, nt, lambda k: move(*lay_set, k).wait_send())
    loop(0, nt, split)

    def back(b):
        lay = jnp.concatenate([layer[slot_ref[b * rpb + r]] for r in range(rpb)], axis=1)
        oa_ref[lev, :, lanes(b)] = lax.dot_general(
            lay, weights(b), (((1,), (1,)), ((), ())), preferred_element_type=jnp.float32
        )

    loop(0, ablk, back)
    oa_swap = pltpu.make_async_remote_copy(
        src_ref=oa_ref.at[lev], dst_ref=oa_ref.at[lev], send_sem=oa_sem.at[0],
        recv_sem=oa_sem.at[1], device_id=partner, device_id_type=MESH,
    )
    oa_swap.start()

    def pass_on(k):
        arrival(*out_set, k).wait_recv()
        forward(k, lev).start()

    loop(1, nt, pass_on)

    def finish(k):
        forward(k, 1 - lev).wait_recv()
        forward(k, lev).wait_send()

    loop(0, nt, finish)
    loop(1, nt, lambda k: move(*out_set, k).wait_send())
    loop(1, nt, lambda k: move(*w_set, k).wait_send())
    oa_swap.wait_send()
    pltpu.make_async_remote_copy(
        src_ref=oa_ref.at[1 - lev], dst_ref=oa_ref.at[1 - lev], send_sem=oa_sem.at[0],
        recv_sem=oa_sem.at[1], device_id=partner, device_id_type=MESH,
    ).wait_recv()


def exchange(slot_of, slot_src, idx, obs, ocn_anom, atm_anom, remap_w, nt, per):
    chunk, parts = 2048, 4
    olev, mem, cells = ocn_anom.shape
    alev, _, acells = atm_anom.shape
    nrem = remap_w.shape[0]
    oblk = cells // 128
    slots = nt * per
    vmem = pl.BlockSpec(memory_space=pltpu.VMEM)
    smem = pl.BlockSpec(memory_space=pltpu.SMEM)
    hbm = pl.BlockSpec(memory_space=pl.ANY)
    dma = pltpu.SemaphoreType.DMA
    f32, bf16, i32 = jnp.float32, jnp.bfloat16, jnp.int32
    return pl.pallas_call(
        functools.partial(main_kernel, nt, per, chunk, parts),
        out_shape=(
            jax.ShapeDtypeStruct((2, nt, per * HALF, 128), bf16),
            jax.ShapeDtypeStruct((2, HALF, acells), f32),
            jax.ShapeDtypeStruct((nt, 8, 128), i32),
        ),
        in_specs=[smem, smem, vmem, vmem, hbm, hbm, hbm],
        out_specs=(vmem,) * 3,
        scratch_shapes=[
            pltpu.VMEM((2, olev, mem, chunk), bf16),
            pltpu.VMEM(atm_anom.shape, bf16),
            pltpu.VMEM(remap_w.shape, bf16),
            pltpu.VMEM((2, HALF, cells), f32),
            pltpu.VMEM((HALF, cells), f32),
            pltpu.VMEM((max(oblk, slots), HALF, 128), bf16),
            pltpu.VMEM((oblk, 8, 128), f32),
            pltpu.VMEM((nt, per * HALF, 128), bf16),
            pltpu.VMEM((nt, per * HALF, 128), bf16),
            pltpu.VMEM((nt, per * 8, 128), bf16),
            pltpu.VMEM((nt, per * 8, 128), bf16),
            pltpu.VMEM((slots, 8, 128), f32),
            pltpu.VMEM((alev, 2 * HALF, 128), bf16),
            pltpu.VMEM((2, nrem, HALF, 128), f32),
            pltpu.VMEM((nrem, HALF, 128), f32),
            pltpu.VMEM((nrem, HALF, 128), bf16),
            pltpu.VMEM((nt, per * HALF, 128), bf16),
            pltpu.SMEM((nt, 8, 128), i32),
            dma((2,)), dma, dma, dma,
            dma((cells // chunk,)), dma((cells // chunk,)),
            dma((parts,)), dma((parts,)), dma((2,)),
        ]
        + [dma((nt,))] * 10,
        compiler_params=pltpu.CompilerParams(
            collective_id=0, has_side_effects=True, vmem_limit_bytes=VLIM
        ),
    )(slot_of, slot_src, idx, obs, ocn_anom, atm_anom, remap_w)


def increment_kernel(per, blk_ref, got_ref, x_ref, innov_ref, band_ref, out_ref, proj):
    i = pl.program_id(0)
    lev, mem, chunk = x_ref.shape
    first = lax.axis_index("lev") * lev

    @pl.when(i == 0)
    def _():
        proj[...] = jnp.zeros_like(proj)

        def put(s, carry):
            blk = blk_ref[s // per, s % per, 1]

            @pl.when(blk >= 0)
            def _():
                at = pl.ds(pl.multiple_of(blk * 128, 128), 128)
                for h in range(2):
                    proj[h * HALF : (h + 1) * HALF, at] += got_ref[h, s].astype(jnp.float32)

            return carry

        lax.fori_loop(0, got_ref.shape[1], put, 0)

    sub = 256

    def piece(j, carry):
        here = pl.ds(pl.multiple_of(j * sub, sub), sub)
        p = proj[:, pl.ds(pl.multiple_of(i * chunk + j * sub, sub), sub)]
        var = jnp.sum(p * p, axis=0, keepdims=True) / (MEM - 1) + 0.1
        scale = innov_ref[:, here] / var / (MEM - 1)
        band = band_ref[:, here].astype(jnp.float32)
        p = p[:mem]
        for level in range(lev):
            cov = jnp.sum(x_ref[level, :, here].astype(jnp.float32) * p, axis=0, keepdims=True)
            dist = jnp.abs((first + level).astype(jnp.float32) - band)
            taper = jnp.maximum(0.0, 1.0 - dist / LTAP)
            out_ref[level : level + 1, here] = taper * cov * scale
        return carry

    lax.fori_loop(0, chunk // sub, piece, 0)


def ocean_increment(blk, got, ocn_anom, innov, band, chunk):
    lev, mem, cells = ocn_anom.shape
    slots = got.shape[1]
    return pl.pallas_call(
        functools.partial(increment_kernel, slots // blk.shape[0]),
        grid=(cells // chunk,),
        in_specs=[
            pl.BlockSpec(memory_space=pltpu.SMEM),
            pl.BlockSpec(got.shape, lambda i: (0, 0, 0, 0)),
            pl.BlockSpec((lev, mem, chunk), lambda i: (0, 0, i)),
            pl.BlockSpec((1, chunk), lambda i: (0, i)),
            pl.BlockSpec((1, chunk), lambda i: (0, i)),
        ],
        out_specs=pl.BlockSpec((lev, chunk), lambda i: (0, i)),
        scratch_shapes=[pltpu.VMEM((2 * HALF, cells), jnp.float32)],
        out_shape=jax.ShapeDtypeStruct((lev, cells), jnp.float32),
        compiler_params=pltpu.CompilerParams(vmem_limit_bytes=VLIM),
        cost_estimate=pl.CostEstimate(
            flops=2 * lev * mem * cells, bytes_accessed=2 * lev * mem * cells, transcendentals=0
        ),
    )(blk, got, ocn_anom, innov.reshape(1, -1), band.reshape(1, -1))


def taper_levels(first, levels, band):
    lvl = (first + jnp.arange(levels, dtype=jnp.int32)).astype(jnp.float32)[:, None]
    return jnp.maximum(0.0, 1.0 - jnp.abs(lvl - band[None, :].astype(jnp.float32)) / LTAP)


def increment(anom, proj, tapered, innov):
    cov = jnp.sum(anom.astype(jnp.float32) * proj[None], axis=1) / (MEM - 1)
    var = jnp.sum(proj * proj, axis=0) / (MEM - 1) + 0.1
    return tapered * cov * (innov / var)[None, :]


def shards(
    atm_anom,
    ocn_anom,
    remap_w,
    rem_tile,
    rem_block,
    obs_weight,
    innov_ocn,
    innov_atm,
    band_ocn,
    band_atm,
):
    nt = lax.axis_size("tiles")
    lev = lax.axis_index("lev")
    alev, _, acells = atm_anom.shape
    nrem = remap_w.shape[0]
    per = max(2, 2 * ((nrem + nt - 1) // nt))
    slots = nt * per
    dest = rem_tile[:, 0]
    match_dest = (dest[:, None] == jnp.arange(nt, dtype=jnp.int32)[None, :]).astype(jnp.int32)
    rank = jnp.sum(jnp.cumsum(match_dest, axis=0) * match_dest, axis=1) - 1
    slot_of = dest * per + rank
    match_slot = (slot_of[None, :] == jnp.arange(slots, dtype=jnp.int32)[:, None]).astype(jnp.int32)
    slot_src = jnp.sum(match_slot * jnp.arange(nrem, dtype=jnp.int32)[None, :], axis=1)
    send_blk = jnp.sum(match_slot * (rem_block + 1)[None, :], axis=1) - 1
    idx = jnp.broadcast_to(send_blk.reshape(nt, per, 1), (nt, per, 128))
    idx = jnp.where(jnp.arange(128) == 0, jnp.maximum(idx, 0), idx)
    idx = jnp.pad(idx, ((0, 0), (0, 8 - per), (0, 0)))
    got, oa2, blk = exchange(
        slot_of, slot_src, idx, obs_weight, ocn_anom, atm_anom, remap_w, nt, per
    )
    got = got.reshape(2, slots, HALF, 128)
    ocn_increment = ocean_increment(blk, got, ocn_anom, innov_ocn, band_ocn, 2048)
    ocn_on_atm = oa2.reshape(2 * HALF, acells)[:MEM]
    taper_atm = taper_levels(lev * alev, alev, band_atm)
    atm_increment = increment(atm_anom, ocn_on_atm, taper_atm, innov_atm)
    return (ocn_increment, atm_increment)


def solution(mesh):
    in_specs = (
        P("lev", None, "tiles"),
        P("lev", None, "tiles"),
        P("tiles", None, None),
        P("tiles", None),
        P("tiles"),
        P("lev", "tiles"),
        P("tiles"),
        P("tiles"),
        P("tiles"),
        P("tiles"),
    )
    out_specs = (P("lev", "tiles"), P("lev", "tiles"))
    return jax.shard_map(shards, mesh=mesh, in_specs=in_specs, out_specs=out_specs, check_vma=False)
```

time: 365 us -> 79.6 us (0.22)
  waiting for transfers between devices: 220 us -> 0 us
  Pallas kernels: 0 us -> 67.9 us
  local copies, waits for them, and re-layouts: 49.3 us -> 4.09 us
  other arithmetic: 31.4 us -> 6.12 us
  starting transfers between devices: 19.9 us -> 0 us
  matrix products: 14.9 us -> 0 us
  between operations: 14.3 us -> 0.72 us
  blocking collectives: 12.6 us -> 0 us
    all_to_all x3 -> x0, waiting for transfers between devices: 194 us -> none  [the longest x1 173 us: shards(): lax.all_to_all(sent, 'tiles', split_axis=0, concat_axis=0, tiled=True)]
    pallas_call x0 -> x2, Pallas kernels: none -> 67.9 us  [the longest x1 50 us: exchange(): pl.pallas_call(functools.partial(main_kernel, nt, per, chunk, parts), out...]
    psum x1 -> x0, waiting for transfers between devices: 25.8 us -> none  [shards(): proj = lax.psum(proj_part, 'lev')]
    all_to_all x3 -> x0, starting transfers between devices: 19.6 us -> none  [the longest x1 6.61 us: shards(): lax.all_to_all(send_blk, 'tiles', split_axis=0, concat_axis=0, tiled=True)]
    unnamed x25 -> x9, local copies, waits for them, and re-layouts: 19.2 us -> 4.01 us
    dot_general x3 -> x0, matrix products: 14.9 us -> none  [the longest x1 8.35 us: shards(): jnp.dot(owner_hot, arrived.reshape(slots, rows * 128), preferred_element_...]
    gather x4 -> x0, local copies, waits for them, and re-layouts: 13.8 us -> none  [the longest x1 8.6 us: shards(): sent = jnp.take(remapped, slot_src, axis=0) * keep]
    psum x1 -> x0, blocking collectives: 12.6 us -> none  [shards(): layer_mean = lax.psum(layer_part, 'lev')]
  transfers between devices with their start and end apart: 4 -> 0, of which waited for: 3 -> 0; matrix products, arithmetic and copies ran while one was open for 8% -> 0% of each run, Pallas kernels for 0% -> 0%
where the time goes in v2:
time: 79.6 us; the launch traced here: 78.8 us
  Pallas kernels  67.9 us (85%)
  other arithmetic  6.12 us (8%)
  local copies, waits for them, and re-layouts  4.09 us (5%)
    pallas_call x1, Pallas kernels, exchange(): pl.pallas_call(functools.partial(main_kernel, nt, per, chunk, parts), out...  50 us
    pallas_call x1, Pallas kernels, ocean_increment(): pl.pallas_call(functools.partial(increment_kernel, slots // blk.shape[0])...  17.9 us
    unnamed x9, local copies, waits for them, and re-layouts  4.01 us

profile of v2, /device:TPU:13, one launch (start us, length us, event | category | flops | bytes accessed | tf_op | source)
XLA Modules:
  0.0 78.8 jit_solution(4107503818536625990)
XLA Ops:
  0.6 0.7 fusion
  1.4 0.1 reduce_window_sum.11
  1.5 0.8 %select_reduce_fusion.2 = s32[64]{0:T(128)S(1)} fusion(s32[64,16]{1,0:T(8,128)S(1)} %reduce_window_sum.11, s32[64]{0:T(128)} %bitcast.11), kind=kLoop, calls=%fused_computation.7 | loop fusion | flops 3008 | bytes 4608 | tf_op jit(solution)/shard_map/reduce_sum | solution.py:432
  2.3 0.7 add_add_fusion
  3.0 0.0 copy-start.3
  3.0 0.7 select_reduce_fusion
  3.7 0.1 sub.30
  3.8 0.7 broadcast_select_fusion.idx_ref
  4.5 4.0 %copy.14.atm_hbm = bf16[8,30,4096]{2,1,0:T(8,128)(2,1)} copy(bf16[8,30,4096]{2,0,1:T(8,128)(2,1)} %param.10) | data formatting | bytes 3932160 | tf_op args[0]
  8.5 0.0 copy-done.3
  8.5 0.0 copy-start
  8.5 50.0 %shard_map.113 = (bf16[2,16,128,128]{3,2,1,0:T(8,128)(2,1)}, f32[2,16,4096]{2,1,0:T(8,128)}, s32[16,8,128]{2,1,0:T(8,128)}) custom-call(s32[64]{0:T(128)} %copy-done.3, s32[128]{0:T(128)} %get-tuple-element.9.src_ref, s32[16,8,128]{2,1,0:T(8,128)} %broadcast_select_fusion.idx_ref, bf16[8,24576]{1,0:T(8,128)(2,1)} %obs_ref.1, bf16[10,30,24576]{2,1,0:T(8,128)(2,1)} %x_ref.1, ...), custom_call_target="tpu_custom_call" | custom-call | tf_op jit(solution)/shard_map/pallas_call | solution.py:298
  58.5 0.0 copy-start.1
  58.5 0.0 copy-start.2
  58.5 1.1 %multiply_reduce_fusion.1 = (f32[4096]{0:T(1024)S(1)}, f32[30,4096]{1,0:T(8,128)S(1)}) fusion(f32[32,4096]{1,0:T(8,128)} %bitcast.7), kind=kLoop, calls=%fused_computation.1 | loop fusion | flops 241664 | bytes 999424 | tf_op jit(solution)/shard_map/reduce_sum | solution.py:408
  59.6 0.0 copy-done
  59.6 0.5 multiply_reduce_fusion
  60.1 0.0 copy-done.1
  60.1 0.0 copy-done.2
  60.1 0.8 multiply_multiply_fusion
  60.9 17.9 %shard_map.114 = f32[10,24576]{1,0:T(8,128)} custom-call(s32[16,8,128]{2,1,0:T(8,128)} %get-tuple-element.5.blk_ref, bf16[2,128,16,128]{3,2,1,0:T(8,128)(2,1)} %bitcast.6, bf16[10,30,24576]{2,1,0:T(8,128)(2,1)} %x_ref.1, f32[1,24576]{1,0:T(1,128)} %bitcast.8, s32[1,24576]{1,0:T(1,128)} %bitcast.9), custom_call_target="tpu_custom_call" | custom-call | flops 14745600 | bytes 14745600 | tf_op jit(solution)/shard_map/pallas_call | solution.py:381
  (6 shorter events, 0.0 us)
Async XLA Ops:
  3.0 5.5 %copy-start.3 = (s32[64]{0:T(128)}, s32[64]{0:T(128)S(1)}, u32[]{:S(2)}) copy-start(s32[64]{0:T(128)S(1)} %get-tuple-element.12.slot_ref) | copy-start | bytes 772
  8.5 51.1 %copy-start = (bf16[8,30,4096]{2,0,1:T(8,128)(2,1)S(1)}, bf16[8,30,4096]{2,0,1:T(8,128)(2,1)}, u32[]{:S(2)}) copy-start(bf16[8,30,4096]{2,0,1:T(8,128)(2,1)} %param.10) | copy-start | bytes 5898244
  58.5 1.6 %copy-start.1 = (f32[4096]{0:T(1024)S(1)}, f32[4096]{0:T(1024)}, u32[]{:S(2)}) copy-start(f32[4096]{0:T(1024)} %param.17) | copy-start | bytes 49156
  58.5 1.6 %copy-start.2 = (s32[4096]{0:T(1024)S(1)}, s32[4096]{0:T(1024)}, u32[]{:S(2)}) copy-start(s32[4096]{0:T(1024)} %param.19) | copy-start | bytes 49156

commit v3 on v2

--- a/solution.py
+++ b/solution.py
@@ -43,18 +43,19 @@
 
 def main_kernel(
     nt, per, chunk, parts,
-    slot_ref, src_ref, idx_ref, obs_ref, ocn_hbm, atm_hbm, rw_hbm,
-    got_ref, oa_ref, blk_ref,
+    slot_ref, src_ref, idx_ref, obs_ref, innov_ref, band_ref, ocn_hbm, atm_hbm, rw_hbm,
+    got_ref, inc_ref, blk_ref,
+    oa_ref,
     ocn, atm, rw, part, peer, layer, obs, lay_out, lay_rx, w_out, w_rx, obs_rx,
-    xs, con, con_peer, summed, out, blk_smem,
+    con, con_peer, summed, out, blk_smem,
     ocn_sem, atm_sem, rw_sem, smem_sem, swap_s, swap_r, con_s, con_r, oa_sem,
     idx_s, idx_r, w_s, w_r, lay_s, lay_r, out_s, out_r, fwd_s, fwd_r,
 ):
     me, lev = lax.axis_index("tiles"), lax.axis_index("lev")
     partner = (me, 1 - lev)
-    alev = atm.shape[0]
+    alev = obs_ref.shape[0]
     nrem = rw.shape[0]
-    ablk = atm.shape[2] // 128
+    ablk = atm.shape[1] // 128
     rpb = nrem // ablk
     nchunk = ocn_hbm.shape[2] // chunk
 
@@ -149,7 +150,6 @@
     layer_sum(nchunk - 1, False)
     atm_copy.start()
     rw_copy.start()
-    xs[...] = jnp.zeros_like(xs)
 
     def mean(i):
         swap(i).wait()
@@ -186,15 +186,13 @@
         return jnp.concatenate([rw[b * rpb + r] for r in range(rpb)], axis=1)
 
     def remap(b):
-        xs[:, :MEM, :] = atm[:, :, lanes(b)]
-        y = jnp.dot(
-            xs[...].reshape(alev * 2 * HALF, 128), weights(b), preferred_element_type=jnp.float32
-        )
-        y = y.astype(jnp.bfloat16).astype(jnp.float32).reshape(alev, 2 * HALF, rpb * 128)
+        y = jnp.dot(atm[:, lanes(b)], weights(b), preferred_element_type=jnp.float32)
+        y = y.astype(jnp.bfloat16).astype(jnp.float32).reshape(MEM, alev, rpb * 128)
         local = jnp.concatenate([obs_rx[slot_ref[b * rpb + r]] for r in range(rpb)], axis=1)
-        total = y[0] * local[0:1]
-        for level in range(1, alev):
-            total = total + y[level] * local[level : level + 1]
+        total = jnp.sum(y * local[None], axis=1)
+        total = jnp.concatenate(
+            [total, jnp.zeros((2 * HALF - MEM, rpb * 128), jnp.float32)], axis=0
+        )
         for r in range(rpb):
             for h in range(2):
                 con[h, b * rpb + r] = total[h * HALF : (h + 1) * HALF, 128 * r : 128 * (r + 1)]
@@ -262,31 +260,48 @@
         recv_sem=oa_sem.at[1], device_id=partner, device_id_type=MESH,
     )
     oa_swap.start()
-
-    def pass_on(k):
-        arrival(*out_set, k).wait_recv()
-        forward(k, lev).start()
-
-    loop(1, nt, pass_on)
-
-    def finish(k):
-        forward(k, 1 - lev).wait_recv()
-        forward(k, lev).wait_send()
-
-    loop(0, nt, finish)
-    loop(1, nt, lambda k: move(*out_set, k).wait_send())
-    loop(1, nt, lambda k: move(*w_set, k).wait_send())
     oa_swap.wait_send()
     pltpu.make_async_remote_copy(
         src_ref=oa_ref.at[1 - lev], dst_ref=oa_ref.at[1 - lev], send_sem=oa_sem.at[0],
         recv_sem=oa_sem.at[1], device_id=partner, device_id_type=MESH,
     ).wait_recv()
-
-
-def exchange(slot_of, slot_src, idx, obs, ocn_anom, atm_anom, remap_w, nt, per):
+    level = lev * alev + lax.broadcasted_iota(jnp.int32, (alev, 128), 0)
+
+    def increment(b):
+        at = lanes(b)
+        halves = [oa_ref[0, :, at], oa_ref[1, :, at]]
+        square = halves[0] * halves[0] + halves[1] * halves[1]
+        var = jnp.sum(square, axis=0, keepdims=True) / (MEM - 1) + 0.1
+        x = atm[:, at].astype(jnp.float32)
+        cov = jnp.zeros((alev, 128), jnp.float32)
+        for m in range(MEM):
+            row = halves[m // HALF][m % HALF : m % HALF + 1]
+            cov = cov + x[m * alev : (m + 1) * alev] * row
+        dist = jnp.abs(level - band_ref[:, at]).astype(jnp.float32)
+        taper = jnp.maximum(0.0, 1.0 - dist / LTAP)
+        inc_ref[:, at] = taper * (cov / (MEM - 1)) * (innov_ref[:, at] / var)
+
+    loop(0, ablk, increment)
+
+    def pass_on(k):
+        arrival(*out_set, k).wait_recv()
+        forward(k, lev).start()
+
+    loop(1, nt, pass_on)
+
+    def finish(k):
+        forward(k, 1 - lev).wait_recv()
+        forward(k, lev).wait_send()
+
+    loop(0, nt, finish)
+    loop(1, nt, lambda k: move(*out_set, k).wait_send())
+    loop(1, nt, lambda k: move(*w_set, k).wait_send())
+
+
+def exchange(slot_of, slot_src, idx, obs, innov, band, ocn_anom, atm_anom, remap_w, nt, per):
     chunk, parts = 2048, 4
     olev, mem, cells = ocn_anom.shape
-    alev, _, acells = atm_anom.shape
+    alev, acells = obs.shape[0], atm_anom.shape[1]
     nrem = remap_w.shape[0]
     oblk = cells // 128
     slots = nt * per
@@ -299,12 +314,13 @@
         functools.partial(main_kernel, nt, per, chunk, parts),
         out_shape=(
             jax.ShapeDtypeStruct((2, nt, per * HALF, 128), bf16),
-            jax.ShapeDtypeStruct((2, HALF, acells), f32),
+            jax.ShapeDtypeStruct((alev, acells), f32),
             jax.ShapeDtypeStruct((nt, 8, 128), i32),
         ),
-        in_specs=[smem, smem, vmem, vmem, hbm, hbm, hbm],
+        in_specs=[smem, smem, vmem, vmem, vmem, vmem, hbm, hbm, hbm],
         out_specs=(vmem,) * 3,
         scratch_shapes=[
+            pltpu.VMEM((2, HALF, acells), f32),
             pltpu.VMEM((2, olev, mem, chunk), bf16),
             pltpu.VMEM(atm_anom.shape, bf16),
             pltpu.VMEM(remap_w.shape, bf16),
@@ -317,7 +333,6 @@
             pltpu.VMEM((nt, per * 8, 128), bf16),
             pltpu.VMEM((nt, per * 8, 128), bf16),
             pltpu.VMEM((slots, 8, 128), f32),
-            pltpu.VMEM((alev, 2 * HALF, 128), bf16),
             pltpu.VMEM((2, nrem, HALF, 128), f32),
             pltpu.VMEM((nrem, HALF, 128), f32),
             pltpu.VMEM((nrem, HALF, 128), bf16),
@@ -331,82 +346,91 @@
         compiler_params=pltpu.CompilerParams(
             collective_id=0, has_side_effects=True, vmem_limit_bytes=VLIM
         ),
-    )(slot_of, slot_src, idx, obs, ocn_anom, atm_anom, remap_w)
-
-
-def increment_kernel(per, blk_ref, got_ref, x_ref, innov_ref, band_ref, out_ref, proj):
-    i = pl.program_id(0)
-    lev, mem, chunk = x_ref.shape
-    first = lax.axis_index("lev") * lev
-
-    @pl.when(i == 0)
-    def _():
-        proj[...] = jnp.zeros_like(proj)
-
-        def put(s, carry):
-            blk = blk_ref[s // per, s % per, 1]
-
-            @pl.when(blk >= 0)
-            def _():
-                at = pl.ds(pl.multiple_of(blk * 128, 128), 128)
-                for h in range(2):
-                    proj[h * HALF : (h + 1) * HALF, at] += got_ref[h, s].astype(jnp.float32)
-
-            return carry
-
-        lax.fori_loop(0, got_ref.shape[1], put, 0)
-
-    sub = 256
-
-    def piece(j, carry):
-        here = pl.ds(pl.multiple_of(j * sub, sub), sub)
-        p = proj[:, pl.ds(pl.multiple_of(i * chunk + j * sub, sub), sub)]
+    )(slot_of, slot_src, idx, obs, innov, band, ocn_anom, atm_anom, remap_w)
+
+
+def increment_kernel(
+    per, blk_ref, got_ref, x_hbm, innov_ref, band_ref, out_ref, proj, x, place, held, sems
+):
+    lev, mem, cells = x_hbm.shape
+    slots = got_ref.shape[1]
+    level = lax.axis_index("lev") * lev + lax.broadcasted_iota(jnp.int32, (lev, 128), 0)
+
+    def clear(o, carry):
+        place[o] = -1
+        return carry
+
+    lax.fori_loop(0, cells // 128, clear, 0)
+
+    def fetch(n):
+        at = pl.ds(pl.multiple_of(held[n] * 128, 128), 128)
+        return pltpu.make_async_copy(x_hbm.at[:, :, at], x.at[n], sems.at[n])
+
+    def put(s, count):
+        blk = blk_ref[s // per, s % per, 1]
+        seen = place[jnp.maximum(blk, 0)]
+        new = jnp.logical_and(blk >= 0, seen < 0)
+
+        @pl.when(new)
+        def _():
+            place[blk] = count
+            held[count] = blk
+            fetch(count).start()
+            for h in range(2):
+                proj[count, h * HALF : (h + 1) * HALF] = got_ref[h, s].astype(jnp.float32)
+
+        @pl.when(jnp.logical_and(blk >= 0, seen >= 0))
+        def _():
+            for h in range(2):
+                proj[seen, h * HALF : (h + 1) * HALF] += got_ref[h, s].astype(jnp.float32)
+
+        return count + new.astype(jnp.int32)
+
+    count = lax.fori_loop(0, slots, put, 0)
+    out_ref[...] = jnp.zeros_like(out_ref)
+
+    def block(n, carry):
+        at = pl.ds(pl.multiple_of(held[n] * 128, 128), 128)
+        p = proj[n]
         var = jnp.sum(p * p, axis=0, keepdims=True) / (MEM - 1) + 0.1
-        scale = innov_ref[:, here] / var / (MEM - 1)
-        band = band_ref[:, here].astype(jnp.float32)
         p = p[:mem]
-        for level in range(lev):
-            cov = jnp.sum(x_ref[level, :, here].astype(jnp.float32) * p, axis=0, keepdims=True)
-            dist = jnp.abs((first + level).astype(jnp.float32) - band)
-            taper = jnp.maximum(0.0, 1.0 - dist / LTAP)
-            out_ref[level : level + 1, here] = taper * cov * scale
+        fetch(n).wait()
+        cov = [
+            jnp.sum(x[n, l].astype(jnp.float32) * p, axis=0, keepdims=True) for l in range(lev)
+        ]
+        cov = jnp.concatenate(cov, axis=0) / (MEM - 1)
+        dist = jnp.abs(level - band_ref[:, at]).astype(jnp.float32)
+        taper = jnp.maximum(0.0, 1.0 - dist / LTAP)
+        out_ref[:, at] = taper * cov * (innov_ref[:, at] / var)
         return carry
 
-    lax.fori_loop(0, chunk // sub, piece, 0)
-
-
-def ocean_increment(blk, got, ocn_anom, innov, band, chunk):
+    lax.fori_loop(0, count, block, 0)
+
+
+def ocean_increment(blk, got, ocn_anom, innov, band):
     lev, mem, cells = ocn_anom.shape
     slots = got.shape[1]
+    vmem = pl.BlockSpec(memory_space=pltpu.VMEM)
     return pl.pallas_call(
         functools.partial(increment_kernel, slots // blk.shape[0]),
-        grid=(cells // chunk,),
         in_specs=[
-            pl.BlockSpec(memory_space=pltpu.SMEM),
-            pl.BlockSpec(got.shape, lambda i: (0, 0, 0, 0)),
-            pl.BlockSpec((lev, mem, chunk), lambda i: (0, 0, i)),
-            pl.BlockSpec((1, chunk), lambda i: (0, i)),
-            pl.BlockSpec((1, chunk), lambda i: (0, i)),
+            pl.BlockSpec(memory_space=pltpu.SMEM), vmem, pl.BlockSpec(memory_space=pl.ANY),
+            vmem, vmem,
         ],
-        out_specs=pl.BlockSpec((lev, chunk), lambda i: (0, i)),
-        scratch_shapes=[pltpu.VMEM((2 * HALF, cells), jnp.float32)],
+        out_specs=vmem,
         out_shape=jax.ShapeDtypeStruct((lev, cells), jnp.float32),
+        scratch_shapes=[
+            pltpu.VMEM((slots, 2 * HALF, 128), jnp.float32),
+            pltpu.VMEM((slots, lev, mem, 128), jnp.bfloat16),
+            pltpu.SMEM((cells // 128,), jnp.int32),
+            pltpu.SMEM((slots,), jnp.int32),
+            pltpu.SemaphoreType.DMA((slots,)),
+        ],
         compiler_params=pltpu.CompilerParams(vmem_limit_bytes=VLIM),
         cost_estimate=pl.CostEstimate(
             flops=2 * lev * mem * cells, bytes_accessed=2 * lev * mem * cells, transcendentals=0
         ),
     )(blk, got, ocn_anom, innov.reshape(1, -1), band.reshape(1, -1))
-
-
-def taper_levels(first, levels, band):
-    lvl = (first + jnp.arange(levels, dtype=jnp.int32)).astype(jnp.float32)[:, None]
-    return jnp.maximum(0.0, 1.0 - jnp.abs(lvl - band[None, :].astype(jnp.float32)) / LTAP)
-
-
-def increment(anom, proj, tapered, innov):
-    cov = jnp.sum(anom.astype(jnp.float32) * proj[None], axis=1) / (MEM - 1)
-    var = jnp.sum(proj * proj, axis=0) / (MEM - 1) + 0.1
-    return tapered * cov * (innov / var)[None, :]
 
 
 def shards(
@@ -422,8 +446,7 @@
     band_atm,
 ):
     nt = lax.axis_size("tiles")
-    lev = lax.axis_index("lev")
-    alev, _, acells = atm_anom.shape
+    acells = atm_anom.shape[2]
     nrem = remap_w.shape[0]
     per = max(2, 2 * ((nrem + nt - 1) // nt))
     slots = nt * per
@@ -437,14 +460,13 @@
     idx = jnp.broadcast_to(send_blk.reshape(nt, per, 1), (nt, per, 128))
     idx = jnp.where(jnp.arange(128) == 0, jnp.maximum(idx, 0), idx)
     idx = jnp.pad(idx, ((0, 0), (0, 8 - per), (0, 0)))
-    got, oa2, blk = exchange(
-        slot_of, slot_src, idx, obs_weight, ocn_anom, atm_anom, remap_w, nt, per
+    rows = atm_anom.transpose(1, 0, 2).reshape(-1, acells)
+    got, atm_increment, blk = exchange(
+        slot_of, slot_src, idx, obs_weight, innov_atm.reshape(1, -1), band_atm.reshape(1, -1),
+        ocn_anom, rows, remap_w, nt, per,
     )
     got = got.reshape(2, slots, HALF, 128)
-    ocn_increment = ocean_increment(blk, got, ocn_anom, innov_ocn, band_ocn, 2048)
-    ocn_on_atm = oa2.reshape(2 * HALF, acells)[:MEM]
-    taper_atm = taper_levels(lev * alev, alev, band_atm)
-    atm_increment = increment(atm_anom, ocn_on_atm, taper_atm, innov_atm)
+    ocn_increment = ocean_increment(blk, got, ocn_anom, innov_ocn, band_ocn)
     return (ocn_increment, atm_increment)
 
 

time: 79.6 us -> 71 us (0.89)
  local copies, waits for them, and re-layouts: 4.09 us -> 0.75 us
  Pallas kernels: 67.9 us -> 65 us
  other arithmetic: 6.12 us -> 3.7 us
    pallas_call x1, Pallas kernels: 17.9 us -> 13.2 us  [ocean_increment(): pl.pallas_call(functools.partial(increment_kernel, slots // blk.shape[0])...]
    unnamed x9 -> x5, local copies, waits for them, and re-layouts: 4.01 us -> 0.67 us
    pallas_call x1, Pallas kernels: 50 us -> 51.8 us  [exchange(): pl.pallas_call(functools.partial(main_kernel, nt, per, chunk, parts), out...]
    reduce_sum x2 -> x0, other arithmetic: 1.58 us -> none  [the longest x1 1.12 us: increment(): var = jnp.sum(proj * proj, axis=0) / (MEM - 1) + 0.1]
where the time goes in v3:
time: 71 us; the launch traced here: 70.1 us
  Pallas kernels  65 us (92%)
  other arithmetic  3.7 us (5%)
  local copies, waits for them, and re-layouts  0.75 us (1%)
    pallas_call x1, Pallas kernels, exchange(): pl.pallas_call(functools.partial(main_kernel, nt, per, chunk, parts), out...  51.8 us
    pallas_call x1, Pallas kernels, ocean_increment(): pl.pallas_call(functools.partial(increment_kernel, slots // blk.shape[0])...  13.2 us

profile of v3, /device:TPU:13, one launch (start us, length us, event | category | flops | bytes accessed | tf_op | source)
XLA Modules:
  0.0 70.1 jit_solution(8270088096210939937)
XLA Ops:
  0.6 0.7 %fusion = s32[64,16]{1,0:T(8,128)S(1)} fusion(s32[64]{0:T(128)} %bitcast.16), kind=kLoop, calls=%fused_computation.6 | loop fusion | flops 2048 | bytes 4352 | tf_op jit(solution)/shard_map/convert_element_type | solution.py:454
  1.4 0.1 reduce_window_sum.11
  1.5 0.8 %select_reduce_fusion.2 = s32[64]{0:T(128)S(1)} fusion(s32[64,16]{1,0:T(8,128)S(1)} %reduce_window_sum.11, s32[64]{0:T(128)} %bitcast.17), kind=kLoop, calls=%fused_computation.4 | loop fusion | flops 3008 | bytes 4608 | tf_op jit(solution)/shard_map/reduce_sum | solution.py:455
  2.3 0.7 add_add_fusion
  3.0 0.0 copy-start.1
  3.0 0.6 select_reduce_fusion
  3.6 0.1 sub.11
  3.7 0.7 %broadcast_select_fusion.idx_ref = s32[16,8,128]{2,1,0:T(8,128)} fusion(s32[16,8]{1,0:T(8,128)S(1)} %sub.11, s32[16,8]{1,0:T(8,128)S(1)} %broadcast_maximum_fusion, pred[128]{0:T(512)(128)(4,1)S(1)} %iota_compare_fusion.2), kind=kLoop, calls=%fused_computation | loop fusion | flops 16384 | bytes 66688 | tf_op jit(solution)/shard_map/jit(_where)/select_n | solution.py:461
  4.4 0.0 copy-done.1
  4.4 51.8 %shard_map.113 = (bf16[2,16,128,128]{3,2,1,0:T(8,128)(2,1)}, f32[8,4096]{1,0:T(8,128)}, s32[16,8,128]{2,1,0:T(8,128)}) custom-call(s32[64]{0:T(128)} %copy-done.1, s32[128]{0:T(128)} %get-tuple-element.9.src_ref, s32[16,8,128]{2,1,0:T(8,128)} %broadcast_select_fusion.idx_ref, bf16[8,24576]{1,0:T(8,128)(2,1)} %obs_ref.1, f32[1,4096]{1,0:T(1,128)} %bitcast.14, ...), custom_call_target="tpu_custom_call" | custom-call | tf_op jit(solution)/shard_map/pallas_call | solution.py:313
  56.3 0.0 copy-start
  56.3 13.2 %shard_map.114 = f32[10,24576]{1,0:T(8,128)} custom-call(s32[16,8,128]{2,1,0:T(8,128)} %get-tuple-element.5.blk_ref, bf16[2,128,16,128]{3,2,1,0:T(8,128)(2,1)} %bitcast.11, bf16[10,30,24576]{2,1,0:T(8,128)(2,1)} %x_hbm.1, f32[1,24576]{1,0:T(1,128)} %bitcast.12, s32[1,24576]{1,0:T(1,128)} %bitcast.13), custom_call_target="tpu_custom_call" | custom-call | flops 14745600 | bytes 14745600 | tf_op jit(solution)/shard_map/pallas_call | solution.py:414
  69.5 0.0 copy-done
  69.5 0.7 copy.13
  (3 shorter events, 0.0 us)
Async XLA Ops:
  3.0 1.4 %copy-start.1 = (s32[64]{0:T(128)}, s32[64]{0:T(128)S(1)}, u32[]{:S(2)}) copy-start(s32[64]{0:T(128)S(1)} %get-tuple-element.10.slot_ref) | copy-start | bytes 772
  56.3 13.2 %copy-start = (f32[8,4096]{1,0:T(8,128)S(1)}, f32[8,4096]{1,0:T(8,128)}, u32[]{:S(2)}) copy-start(f32[8,4096]{1,0:T(8,128)} %get-tuple-element.15) | copy-start | bytes 393220
